TPU v7x, 256 devices: a whole 4x4x8 slice. The times are simulated.
256 devices in a mesh: inst: 32 (over y, z_hi, x), tp: 8 (over z_lo, core).
Axes of the slice: x: 4, y: 4, z: 8 (z_hi: 2, z_lo: 4; z = z_hi * 4 + z_lo), core: 2. Of those that a mesh axis runs over, the one named last changes fastest.
Arguments:
- new_queries: bfloat16 [512, 2, 8192], P(('inst', 'tp')), may hold values from -6 to 6
- new_keys: bfloat16 [512, 2, 1024], P(('inst', 'tp')), may hold values from -6 to 6
- new_values: bfloat16 [512, 2, 1024], P(('inst', 'tp')), may hold values from -6 to 6
- key_pool: bfloat16 [2048, 128, 1024], P('inst', None, 'tp'), may hold values from -6 to 6
- value_pool: bfloat16 [2048, 128, 1024], P('inst', None, 'tp'), may hold values from -6 to 6
- lengths: int32 [512], replicated, may hold values from 1 to 512
- page_table: int32 [512, 4], P('inst'), may hold values from 0 to 63, as said below
- mig_row: int32 [352], replicated, may hold values from 0 to 511, as said below
- mig_source: int32 [352], replicated, may hold values from 0 to 31, as said below
- mig_pages: int32 [352, 4], replicated, may hold values from 0 to 63, as said below
Outputs:
- attention: bfloat16 [512, 2, 8192], P(('inst', 'tp'))
- key_moved: bfloat16 [2048, 128, 1024], P('inst', None, 'tp')
- value_moved: bfloat16 [2048, 128, 1024], P('inst', None, 'tp')
Inputs may be any that keep to these rules, and one draw needn't show every extreme that they name: `page_table`: the 4 pages of the 16 rows of one instance are its 64 pool pages, each once. `mig_row`: the rows are distinct; every instance is the target of exactly 11 migrations. `mig_source`: every instance is the source of exactly 11 migrations, to distinct instances, never to itself. `mig_pages`: the pages of the migrations leaving one instance are distinct.
All inputs are finite; a program needn't handle non-finite values.
Results may differ from a plain program's by a relative error of at most 0.0049.
Values may be sent and summed in bfloat16 or wider, within the bound.
No kernel may reach another device: no remote copies, remote signals or barrier semaphores. Data moves between devices by JAX's collectives and lax.ppermute only.
A program may use at most 128 MiB of HBM per device.

v0:
```python
import math

import jax
import jax.numpy as jnp
from jax import lax
from jax.sharding import PartitionSpec as P

HD = 128


def attend(queries, fresh_keys, fresh_values, cache_keys, cache_values, row_lengths):
    row_count = queries.shape[0]
    groups = fresh_keys.shape[-1] // HD
    group_size = queries.shape[-1] // fresh_keys.shape[-1]
    query_b = queries.reshape(row_count, 2, groups, group_size, HD)
    keys_c = cache_keys.reshape(row_count, -1, groups, HD)
    values_c = cache_values.reshape(row_count, -1, groups, HD)
    keys_n = fresh_keys.reshape(row_count, 2, groups, HD)
    values_n = fresh_values.reshape(row_count, 2, groups, HD)
    score_scale = 1.0 / math.sqrt(HD)
    cache_scores = (
        jnp.einsum("rskgd,rtkd->rskgt", query_b, keys_c, preferred_element_type=jnp.float32)
        * score_scale
    )
    positions = jnp.arange(keys_c.shape[1], dtype=jnp.int32)
    visible = positions[None, :] < row_lengths[:, None]
    cache_scores = jnp.where(visible[:, None, None, None, :], cache_scores, -jnp.inf)
    fresh_scores = (
        jnp.einsum("rskgd,rjkd->rskgj", query_b, keys_n, preferred_element_type=jnp.float32)
        * score_scale
    )
    steps_idx = jnp.arange(2, dtype=jnp.int32)
    causal = steps_idx[None, :] <= steps_idx[:, None]
    fresh_scores = jnp.where(causal[None, :, None, None, :], fresh_scores, -jnp.inf)
    row_max = jnp.maximum(jnp.max(cache_scores, axis=-1), jnp.max(fresh_scores, axis=-1))[..., None]
    cache_exp = jnp.exp(cache_scores - row_max)
    fresh_exp = jnp.exp(fresh_scores - row_max)
    weight_sum = jnp.sum(cache_exp, axis=-1, keepdims=True) + jnp.sum(
        fresh_exp, axis=-1, keepdims=True
    )
    cache_weights = (cache_exp / weight_sum).astype(jnp.bfloat16)
    fresh_weights = (fresh_exp / weight_sum).astype(jnp.bfloat16)
    mixed = jnp.einsum(
        "rskgt,rtkd->rskgd", cache_weights, values_c, preferred_element_type=jnp.float32
    )
    mixed = mixed + jnp.einsum(
        "rskgj,rjkd->rskgd", fresh_weights, values_n, preferred_element_type=jnp.float32
    )
    return mixed.astype(jnp.bfloat16).reshape(row_count, 2, -1)


def migrate_pages(
    key_pool,
    value_pool,
    page_table,
    mig_source,
    mig_pages,
    incoming,
    outgoing,
    in_rows,
    targets_out,
):
    inst_count = lax.axis_size("inst")
    pool_size = key_pool.shape[0]
    page_count = mig_pages.shape[1]
    send_pages = mig_pages[outgoing]
    blank = jnp.zeros((inst_count, page_count) + key_pool.shape[1:], jnp.bfloat16)
    key_slots = blank.at[targets_out].set(key_pool[send_pages])
    value_slots = blank.at[targets_out].set(value_pool[send_pages])
    key_recv, value_recv = (
        lax.all_to_all(key_slots, "inst", split_axis=0, concat_axis=0, tiled=True),
        lax.all_to_all(value_slots, "inst", split_axis=0, concat_axis=0, tiled=True),
    )
    destination = jnp.full((inst_count, page_count), pool_size, jnp.int32)
    destination = destination.at[mig_source[incoming]].set(page_table[in_rows]).reshape(-1)
    flat_shape = (-1,) + key_pool.shape[1:]
    key_moved = key_pool.at[destination].set(key_recv.reshape(flat_shape), mode="drop")
    value_moved = value_pool.at[destination].set(value_recv.reshape(flat_shape), mode="drop")
    return (key_moved, value_moved)


def body(
    new_queries,
    new_keys,
    new_values,
    key_pool,
    value_pool,
    lengths,
    page_table,
    mig_row,
    mig_source,
    mig_pages,
):
    own_inst = lax.axis_index("inst")
    inst_count = lax.axis_size("inst")
    rows_here = page_table.shape[0]
    move_count = mig_source.shape[0] // inst_count
    queries, fresh_keys, fresh_values = (
        lax.all_to_all(new_queries, "tp", split_axis=2, concat_axis=0, tiled=True),
        lax.all_to_all(new_keys, "tp", split_axis=2, concat_axis=0, tiled=True),
        lax.all_to_all(new_values, "tp", split_axis=2, concat_axis=0, tiled=True),
    )
    row_lengths = lax.dynamic_slice_in_dim(lengths, own_inst * rows_here, rows_here)
    incoming = jnp.nonzero(mig_row // rows_here == own_inst, size=move_count)[0]
    outgoing = jnp.nonzero(mig_source == own_inst, size=move_count)[0]
    in_rows = mig_row[incoming] - own_inst * rows_here
    targets_out = mig_row[outgoing] // rows_here
    key_moved, value_moved = migrate_pages(
        key_pool,
        value_pool,
        page_table,
        mig_source,
        mig_pages,
        incoming,
        outgoing,
        in_rows,
        targets_out,
    )
    heads_out = attend(
        queries,
        fresh_keys,
        fresh_values,
        key_moved[page_table],
        value_moved[page_table],
        row_lengths,
    )
    attention = lax.all_to_all(heads_out, "tp", split_axis=0, concat_axis=2, tiled=True)
    return (attention, key_moved, value_moved)


def solution(mesh):
    placed = (
        P(("inst", "tp"), None, None),
        P(("inst", "tp"), None, None),
        P(("inst", "tp"), None, None),
        P("inst", None, "tp"),
        P("inst", None, "tp"),
        P(),
        P("inst", None),
        P(),
        P(),
        P(),
    )
    return jax.shard_map(
        body,
        mesh=mesh,
        in_specs=placed,
        out_specs=(P(("inst", "tp"), None, None), P("inst", None, "tp"), P("inst", None, "tp")),
        check_vma=False,
    )
```

profile of v0, /device:TPU:1, one launch (start us, length us, event | category | flops | bytes accessed | tf_op | source)
XLA Modules:
  0.0 315.8 jit_solution(8879346814405586064)
XLA Ops:
  0.6 3.3 %copy.55 = bf16[64,128,128]{2,1,0:T(8,128)(2,1)} copy(bf16[64,128,128]{2,1,0:T(8,128)(2,1)} %param.13) | data formatting | bytes 4194304
  5.1 1.3 reshape.552
  6.4 7.4 %all-to-all-start.3 = ((bf16[8,2,256]{2,1,0:T(2,128)(2,1)}), bf16[8,2,256]{2,1,0:T(2,128)(2,1)S(1)}, u32[]{:S(2)}, u32[]{:S(2)}) async-start(bf16[8,2,256]{2,1,0:T(2,128)(2,1)} %reshape.552), calls=%async_computation.3 | async-start | bytes 16384 | tf_op jit(solution)/shard_map/all_to_all | solution.py:100
  15.0 3.8 %scatter_custom_fusion.2 = s32[11]{0:T(128)S(1)} fusion(s32[352]{0:T(512)S(1)} %compare_select_fusion.2, s32[352]{0:T(512)S(1)} %ne.91, s32[]{:T(128)} %constant.84.clone.1), kind=kCustom, calls=%fused_computation.89 | custom fusion | flops 352 | bytes 48 | tf_op jit(solution)/shard_map/scatter-add | solution.py:105
  21.2 1.3 reshape.550
  22.5 5.1 %all-to-all-start.4 = ((bf16[8,2,256]{2,1,0:T(2,128)(2,1)}), bf16[8,2,256]{2,1,0:T(2,128)(2,1)}, u32[]{:S(2)}, u32[]{:S(2)}) async-start(bf16[8,2,256]{2,1,0:T(2,128)(2,1)} %reshape.550), calls=%async_computation.4 | async-start | bytes 16384 | tf_op jit(solution)/shard_map/all_to_all | solution.py:101
  27.6 1.2 gather_fusion.2
  28.8 6.8 %copy.36 = bf16[2,2,8192]{1,0,2:T(2,128)(2,1)} copy(bf16[2,2,8192]{2,1,0:T(2,128)(2,1)S(1)} %copy-done.4) | data formatting | bytes 131072 | tf_op args[0]
  35.6 7.8 %reshape.554 = bf16[8,2,2048]{2,1,0:T(2,128)(2,1)} reshape(bf16[8192,2,2]{2,1,0:T(2,128)(2,1)} %bitcast.121) | data formatting | bytes 131072
  43.4 2.4 gather_fusion.6
  45.8 5.1 %all-to-all-start.2 = ((bf16[8,2,2048]{2,1,0:T(2,128)(2,1)}), bf16[8,2,2048]{2,1,0:T(2,128)(2,1)}, u32[]{:S(2)}, u32[]{:S(2)}) async-start(bf16[8,2,2048]{2,1,0:T(2,128)(2,1)} %reshape.554), calls=%async_computation.2 | async-start | bytes 131072 | tf_op jit(solution)/shard_map/all_to_all | solution.py:99
  51.5 3.0 broadcast_in_dim.45.clone
  54.6 5.1 %scatter_fusion.2 = bf16[32,4,128,128]{3,2,1,0:T(8,128)(2,1)} fusion(bf16[32,4,128,128]{3,2,1,0:T(8,128)(2,1)} %broadcast_in_dim.45.clone, s32[11]{0:T(128)S(1)} %fusion.25, bf16[11,4,128,128]{3,2,1,0:T(8,128)(2,1)S(1)} %bitcast.123), kind=kCustom, calls=%fused_computation.14 | custom fusion | bytes 4325420 | tf_op jit(solution)/shard_map/scatter | solution.py:68
  59.6 11.1 %all-to-all-start.1 = ((bf16[32,4,128,128]{3,2,1,0:T(8,128)(2,1)}), bf16[32,4,128,128]{3,2,1,0:T(8,128)(2,1)}, u32[]{:S(2)}, u32[]{:S(2)}) async-start(bf16[32,4,128,128]{3,2,1,0:T(8,128)(2,1)} %scatter_fusion.2), calls=%async_computation.1 | async-start | bytes 8388608 | tf_op jit(solution)/shard_map/all_to_all | solution.py:71
  71.6 3.0 broadcast_in_dim.45.clone.1
  74.6 5.0 %scatter_fusion = bf16[32,4,128,128]{3,2,1,0:T(8,128)(2,1)} fusion(bf16[32,4,128,128]{3,2,1,0:T(8,128)(2,1)} %broadcast_in_dim.45.clone.1, s32[11]{0:T(128)S(1)} %fusion.25, bf16[11,4,128,128]{3,2,1,0:T(8,128)(2,1)S(1)} %bitcast.124), kind=kCustom, calls=%fused_computation.12 | custom fusion | bytes 4325420 | tf_op jit(solution)/shard_map/scatter | solution.py:69
  79.5 45.7 %all-to-all-done.1 = bf16[32,4,128,128]{3,2,1,0:T(8,128)(2,1)} async-done(((bf16[32,4,128,128]{3,2,1,0:T(8,128)(2,1)}), bf16[32,4,128,128]{3,2,1,0:T(8,128)(2,1)}, u32[]{:S(2)}, u32[]{:S(2)}) %all-to-all-start.1) | async-done | bytes 4194336 | tf_op jit(solution)/shard_map/all_to_all | solution.py:71
  125.2 31.7 %all-to-all-start = ((bf16[32,4,128,128]{3,2,1,0:T(8,128)(2,1)}), bf16[32,4,128,128]{3,2,1,0:T(8,128)(2,1)}, u32[]{:S(2)}, u32[]{:S(2)}) async-start(bf16[32,4,128,128]{3,2,1,0:T(8,128)(2,1)} %scatter_fusion), calls=%async_computation | async-start | bytes 8388608 | tf_op jit(solution)/shard_map/all_to_all | solution.py:72
  158.3 4.0 %scatter_custom_fusion = s32[11]{0:T(128)S(1)} fusion(s32[352]{0:T(512)S(1)} %compare_select_fusion.3, s32[352]{0:T(512)} %copy-done.11, s32[]{:T(128)} %constant.84.clone.1), kind=kCustom, calls=%fused_computation.91 | custom fusion | flops 352 | bytes 556 | tf_op jit(solution)/shard_map/scatter-add | solution.py:104
  164.5 0.8 scatter_custom_fusion.1
  166.6 1.1 reshape.553
  168.0 1.8 reshape.551
  170.2 10.7 %reshape.555 = bf16[8192,2,2]{2,1,0:T(2,128)(2,1)} reshape(bf16[8,2,2048]{2,1,0:T(2,128)(2,1)} %all-to-all-done.2) | data formatting | bytes 131072
  180.9 9.7 %copy.37 = bf16[2,2,8,1024]{3,1,0,2:T(2,128)(2,1)S(1)} copy(bf16[2,2,8,1024]{1,0,3,2:T(2,128)(2,1)} %bitcast.120) | data formatting | bytes 131072 | tf_op jit(solution)/shard_map/all_to_all | solution.py:99
  191.1 17.9 %scatter_fusion.3 = bf16[64,128,128]{2,1,0:T(8,128)(2,1)} fusion(bf16[64,128,128]{2,1,0:T(8,128)(2,1)} %copy.55, s32[128]{0:T(128)S(1)} %fusion.23, bf16[128,128,128]{2,1,0:T(8,128)(2,1)} %bitcast.22), kind=kCustom, calls=%fused_computation.15 | custom fusion | bytes 12583424 | tf_op jit(solution)/shard_map/scatter | solution.py:77
  209.0 3.7 %gather_fusion.7 = bf16[64,128,128]{2,1,0:T(8,128)(2,1)} fusion(bf16[64,128,128]{2,1,0:T(8,128)(2,1)} %scatter_fusion.3, s32[1024]{0:T(1024)S(1)} %pad_clamp_fusion), kind=kCustom, calls=%fused_computation.8 | custom fusion | bytes 4194560 | tf_op jit(solution)/shard_map/gather | solution.py:123
  212.7 2.3 fusion.33
  215.4 6.2 %all-to-all-done = bf16[32,4,128,128]{3,2,1,0:T(8,128)(2,1)} async-done(((bf16[32,4,128,128]{3,2,1,0:T(8,128)(2,1)}), bf16[32,4,128,128]{3,2,1,0:T(8,128)(2,1)}, u32[]{:S(2)}, u32[]{:S(2)}) %all-to-all-start) | async-done | bytes 4194336 | tf_op jit(solution)/shard_map/all_to_all | solution.py:72
  221.7 12.8 %scatter_fusion.1 = bf16[64,128,128]{2,1,0:T(8,128)(2,1)S(1)} fusion(bf16[64,128,128]{2,1,0:T(8,128)(2,1)S(1)} %copy.56, s32[128]{0:T(128)S(1)} %fusion.23, bf16[128,128,128]{2,1,0:T(8,128)(2,1)} %bitcast.17), kind=kCustom, calls=%fused_computation.13 | custom fusion | bytes 12583424 | tf_op jit(solution)/shard_map/scatter | solution.py:78
  234.5 2.2 gather_fusion.5
  236.9 2.1 fusion.4
  239.0 76.1 %all_to_all.73 = bf16[16,2,1024]{2,1,0:T(2,128)(2,1)S(1)} all-to-all(bf16[16,2,1024]{2,1,0:T(2,128)(2,1)S(1)} %reshape.395), channel_id=1, replica_groups=mesh['inst'=32,'tp'=8] {'tp'}, dimensions={0} | all-to-all | bytes 131072 | tf_op jit(solution)/shard_map/all_to_all | solution.py:127
  (89 shorter events, 13.3 us)
Async XLA Ops:
  0.6 3.3 %copy-start.3 = (bf16[64,128,128]{2,1,0:T(8,128)(2,1)S(1)}, bf16[64,128,128]{2,1,0:T(8,128)(2,1)}, u32[]{:S(2)}) copy-start(bf16[64,128,128]{2,1,0:T(8,128)(2,1)} %param.14) | copy-start | bytes 6291460
  4.0 0.7 copy-start.7
  4.0 9.8 %copy-start.1 = (s32[352]{0:T(512)S(1)}, s32[352]{0:T(512)}, u32[]{:S(2)}) copy-start(s32[352]{0:T(512)} %param.18) | copy-start | bytes 4228
  4.0 15.8 %copy-start.10 = (s32[352,4]{0,1:T(4,128)S(1)}, s32[352,4]{0,1:T(4,128)}, u32[]{:S(2)}) copy-start(s32[352,4]{0,1:T(4,128)} %param.19) | copy-start | bytes 16900
  4.0 16.8 %copy-start.8 = (bf16[2,2,1024]{2,1,0:T(2,128)(2,1)S(1)}, bf16[2,2,1024]{2,1,0:T(2,128)(2,1)}, u32[]{:S(2)}) copy-start(bf16[2,2,1024]{2,1,0:T(2,128)(2,1)} %param.12) | copy-start | bytes 24580
  4.6 22.9 %copy-start = (s32[352]{0:T(512)S(1)}, s32[352]{0:T(512)}, u32[]{:S(2)}) copy-start(s32[352]{0:T(512)} %param.17) | copy-start | bytes 4228
  4.7 24.1 %copy-start.4 = (bf16[2,2,8192]{2,1,0:T(2,128)(2,1)S(1)}, bf16[2,2,8192]{2,1,0:T(2,128)(2,1)}, u32[]{:S(2)}) copy-start(bf16[2,2,8192]{2,1,0:T(2,128)(2,1)} %param.10) | copy-start | bytes 196612
  6.4 16.1 %all-to-all-start.3 = ((bf16[8,2,256]{2,1,0:T(2,128)(2,1)}), bf16[8,2,256]{2,1,0:T(2,128)(2,1)S(1)}, u32[]{:S(2)}, u32[]{:S(2)}) async-start(bf16[8,2,256]{2,1,0:T(2,128)(2,1)} %reshape.552), calls=%async_computation.3 | async-start | bytes 16384 | tf_op jit(solution)/shard_map/all_to_all | solution.py:100
  15.0 4.0 %copy-start.11 = (s32[352]{0:T(512)}, s32[352]{0:T(512)S(1)}, u32[]{:S(2)}) copy-start(s32[352]{0:T(512)S(1)} %ne.91) | copy-start | bytes 4228
  22.5 13.1 %copy-start.5 = (bf16[8,2,256]{2,1,0:T(2,128)(2,1)}, bf16[8,2,256]{2,1,0:T(2,128)(2,1)S(1)}, u32[]{:S(2)}) copy-start(bf16[8,2,256]{2,1,0:T(2,128)(2,1)S(1)} %all-to-all-done.3) | copy-start | bytes 24580
  22.5 23.3 %all-to-all-start.4 = ((bf16[8,2,256]{2,1,0:T(2,128)(2,1)}), bf16[8,2,256]{2,1,0:T(2,128)(2,1)}, u32[]{:S(2)}, u32[]{:S(2)}) async-start(bf16[8,2,256]{2,1,0:T(2,128)(2,1)} %reshape.550), calls=%async_computation.4 | async-start | bytes 16384 | tf_op jit(solution)/shard_map/all_to_all | solution.py:101
  45.8 13.8 %all-to-all-start.2 = ((bf16[8,2,2048]{2,1,0:T(2,128)(2,1)}), bf16[8,2,2048]{2,1,0:T(2,128)(2,1)}, u32[]{:S(2)}, u32[]{:S(2)}) async-start(bf16[8,2,2048]{2,1,0:T(2,128)(2,1)} %reshape.554), calls=%async_computation.2 | async-start | bytes 131072 | tf_op jit(solution)/shard_map/all_to_all | solution.py:99
  59.6 65.6 %all-to-all-start.1 = ((bf16[32,4,128,128]{3,2,1,0:T(8,128)(2,1)}), bf16[32,4,128,128]{3,2,1,0:T(8,128)(2,1)}, u32[]{:S(2)}, u32[]{:S(2)}) async-start(bf16[32,4,128,128]{3,2,1,0:T(8,128)(2,1)} %scatter_fusion.2), calls=%async_computation.1 | async-start | bytes 8388608 | tf_op jit(solution)/shard_map/all_to_all | solution.py:71
  79.5 84.9 %copy-start.9 = (s32[16,4]{0,1:T(4,128)S(1)}, s32[16,4]{0,1:T(4,128)}, u32[]{:S(2)}) copy-start(s32[16,4]{0,1:T(4,128)} %param.16) | copy-start | bytes 772
  79.5 87.0 %copy-start.6 = (bf16[8,2,256]{2,1,0:T(2,128)(2,1)S(1)}, bf16[8,2,256]{2,1,0:T(2,128)(2,1)}, u32[]{:S(2)}) copy-start(bf16[8,2,256]{2,1,0:T(2,128)(2,1)} %copy-done.5) | copy-start | bytes 24580
  125.2 96.4 %all-to-all-start = ((bf16[32,4,128,128]{3,2,1,0:T(8,128)(2,1)}), bf16[32,4,128,128]{3,2,1,0:T(8,128)(2,1)}, u32[]{:S(2)}, u32[]{:S(2)}) async-start(bf16[32,4,128,128]{3,2,1,0:T(8,128)(2,1)} %scatter_fusion), calls=%async_computation | async-start | bytes 8388608 | tf_op jit(solution)/shard_map/all_to_all | solution.py:72
  234.5 2.2 copy-start.2
where the time goes:
time: 318 us; the launch traced here: 316 us
  local copies, waits for them, and re-layouts  109 us (34%)
  blocking collectives  76.1 us (24%)
  starting transfers between devices  60.4 us (19%)
  waiting for transfers between devices  51.9 us (16%)
  other arithmetic  12.7 us (4%)
  matrix products  5.04 us (2%)
    all_to_all x1, blocking collectives, body(): lax.all_to_all(heads_out, 'tp', split_axis=0, concat_axis=2, tiled=True)  76.1 us
    all_to_all x1, waiting for transfers between devices, migrate_pages(): lax.all_to_all(key_slots, 'inst', split_axis=0, concat_axis=0, tiled=True)  45.7 us
    unnamed x37, local copies, waits for them, and re-layouts  35.9 us
    all_to_all x1, starting transfers between devices, migrate_pages(): lax.all_to_all(value_slots, 'inst', split_axis=0, concat_axis=0, tiled=True)  31.7 us
    scatter x1, local copies, waits for them, and re-layouts, migrate_pages(): key_pool.at[destination].set(key_recv.reshape(flat_shape), mode='drop')  17.9 us
    scatter x1, local copies, waits for them, and re-layouts, migrate_pages(): value_pool.at[destination].set(value_recv.reshape(flat_shape), mode='drop')  12.8 us
    all_to_all x1, starting transfers between devices, migrate_pages(): lax.all_to_all(key_slots, 'inst', split_axis=0, concat_axis=0, tiled=True)  11.1 us
    all_to_all x1, local copies, waits for them, and re-layouts, body(): lax.all_to_all(new_queries, 'tp', split_axis=2, concat_axis=0, tiled=True)  9.71 us
  transfers between devices with their start and end apart: 5, of which 2 were waited for; matrix products, arithmetic and copies ran while one was open for 33% of the time, Pallas kernels for 0%

commit v1 on v0

v1 whole, which is shorter than its diff:
```python
import functools
import math

import jax
import jax.numpy as jnp
from jax import lax
from jax.experimental import pallas as pl
from jax.experimental.pallas import tpu as pltpu
from jax.sharding import Mesh
from jax.sharding import PartitionSpec as P

HD = 128
PAGE = 128
MAXP = 4
ROWS = 16
POOL = 64
MOVES = 11
MIGS = 352
NX = 4
NZ = 2
TP = 8
GROUP = 8
SPREAD = 16
PIECES = SPREAD * MOVES
WIDTH = 256
CAPS = (96, 112, 144, PIECES)
HALVES = 1
PR = PAGE * MAXP // SPREAD // HALVES
QKV = 48
VMEM = pltpu.VMEM
SMEM = pltpu.SMEM
LIMIT = pltpu.CompilerParams(vmem_limit_bytes=40 * 1024 * 1024)


def spec(space):
    return pl.BlockSpec(memory_space=space)


def cost(bytes_accessed, flops=0):
    return pl.CostEstimate(flops=flops, bytes_accessed=bytes_accessed, transcendentals=0)


def place_of(inst):
    half = (inst >> 2) & 1
    place = ((inst >> 3) << 2) | (inst & 3)
    return half, place


def plan_kernel(own_ref, row_ref, src_ref, pages_ref, table_ref, out_ref):
    own = own_ref[0]
    half, _ = place_of(own)
    sub = lax.broadcasted_iota(jnp.int32, (MIGS, MIGS), 0)
    lane = lax.broadcasted_iota(jnp.int32, (MIGS, MIGS), 1)

    def to_column(row):
        spread = jnp.where(sub == lane, row.astype(jnp.float32), 0.0)
        return jnp.sum(spread, axis=1, keepdims=True).astype(jnp.int32)

    def rank(same):
        counted = jnp.where((lane < sub) & same, 1.0, 0.0)
        return jnp.sum(counted, axis=1, keepdims=True).astype(jnp.int32)

    row_r, src_r = row_ref[...], src_ref[...]
    row_c, src_c = to_column(row_r), to_column(src_r)
    tgt_r, tgt_c = row_r >> 4, row_c >> 4
    sh_r, _ = place_of(src_r)
    th_r, _ = place_of(tgt_r)
    sh_c, sp_c = place_of(src_c)
    th_c, tp_c = place_of(tgt_c)
    rank_src = rank(src_c == src_r)
    rank_tgt = rank(tgt_c == tgt_r)
    rank_cross = rank((sh_c == sh_r) & (sh_r != th_r))
    src_place = sp_c * MOVES + rank_src
    final_place = tp_c * MOVES + rank_tgt
    col = lax.broadcasted_iota(jnp.int32, (1, WIDTH), 1)
    message, page = col >> 2, col & 3

    def pick(chosen, value):
        picked = jnp.where(chosen, value.astype(jnp.float32), 0.0)
        return jnp.sum(picked, axis=0, keepdims=True).astype(jnp.int32)

    leaves = (sh_c == half) & (th_c != half)
    out_ref[0:1, :] = pick(leaves & (rank_cross == col), src_place)
    origin = jnp.where(sh_c == half, src_place, PIECES + rank_cross)
    out_ref[1:2, :] = pick((th_c == half) & (final_place == col), origin)
    pages = pages_ref[...]
    by_page = pages[:, 3:4]
    for j in range(MAXP - 1):
        by_page = jnp.where(page == j, pages[:, j : j + 1], by_page)
    out_ref[2:3, :] = pick((src_c == own) & (rank_src == message), by_page)
    arrival = pick((tgt_c == own) & (rank_tgt == message), row_c & (ROWS - 1))
    table = table_ref[...]
    by_page = table[:, 3:4]
    for j in range(MAXP - 1):
        by_page = jnp.where(page == j, table[:, j : j + 1], by_page)
    row_id = lax.broadcasted_iota(jnp.int32, (ROWS, WIDTH), 0)
    out_ref[3:4, :] = pick(row_id == arrival, by_page)
    out_ref[4:5, :] = arrival
    out_ref[5:6, :] = pick(leaves & (col >= 0), jnp.ones_like(src_place))
    out_ref[6:8, :] = jnp.zeros((2, WIDTH), jnp.int32)


def make_plan(own, mig_row, mig_source, mig_pages, page_table):
    return pl.pallas_call(
        plan_kernel,
        out_shape=jax.ShapeDtypeStruct((8, WIDTH), jnp.int32),
        in_specs=[spec(SMEM), spec(VMEM), spec(VMEM), spec(VMEM), spec(VMEM)],
        out_specs=spec(VMEM),
        compiler_params=LIMIT,
        cost_estimate=cost(100_000),
    )(own, mig_row.reshape(1, MIGS), mig_source.reshape(1, MIGS), mig_pages, page_table)


def pack_kernel(q_ref, k_ref, v_ref, out_ref, scratch):
    scratch[...] = jnp.zeros_like(scratch)
    for d in range(TP):
        for r in range(2):
            for g in range(GROUP):
                head = d * GROUP + g
                piece = q_ref[r, :, head * HD : (head + 1) * HD]
                scratch[d, r, 2 * g : 2 * g + 2, :] = piece.astype(jnp.float32)
            scratch[d, r, 16:18, :] = k_ref[r, :, d * HD : (d + 1) * HD].astype(jnp.float32)
            scratch[d, r, 32:34, :] = v_ref[r, :, d * HD : (d + 1) * HD].astype(jnp.float32)
    out_ref[...] = scratch[...].astype(jnp.bfloat16)


def pack(new_queries, new_keys, new_values):
    return pl.pallas_call(
        pack_kernel,
        out_shape=jax.ShapeDtypeStruct((TP, 2, QKV, HD), jnp.bfloat16),
        in_specs=[spec(VMEM)] * 3,
        out_specs=spec(VMEM),
        scratch_shapes=[pltpu.VMEM((TP, 2, QKV, HD), jnp.float32)],
        compiler_params=LIMIT,
        cost_estimate=cost(400_000),
    )(new_queries, new_keys, new_values)


def unpack_kernel(in_ref, out_ref):
    for d in range(TP):
        for r in range(2):
            block = in_ref[d, r].astype(jnp.float32)
            for g in range(GROUP):
                head = d * GROUP + g
                piece = block[2 * g : 2 * g + 2, :]
                out_ref[r, :, head * HD : (head + 1) * HD] = piece.astype(jnp.bfloat16)


def unpack(received):
    return pl.pallas_call(
        unpack_kernel,
        out_shape=jax.ShapeDtypeStruct((2, 2, TP * GROUP * HD), jnp.bfloat16),
        in_specs=[spec(VMEM)],
        out_specs=spec(VMEM),
        compiler_params=LIMIT,
        cost_estimate=cost(200_000),
    )(received)


def send_kernel(part, plan_ref, pool_ref, out_ref, sem):
    copies = []
    for m in range(MOVES):
        for j in range(MAXP):
            copies.append(
                pltpu.make_async_copy(
                    pool_ref.at[plan_ref[2, m * MAXP + j], :, part],
                    out_ref.at[MAXP * j : MAXP * (j + 1), m],
                    sem.at[m * MAXP + j],
                )
            )
    for copy in copies:
        copy.start()
    for copy in copies:
        copy.wait()


def outgoing(plan, pool, part):
    return pl.pallas_call(
        functools.partial(send_kernel, part),
        out_shape=jax.ShapeDtypeStruct((SPREAD, MOVES, PR, HD), jnp.bfloat16),
        in_specs=[spec(SMEM), spec(pl.ANY)],
        out_specs=spec(VMEM),
        scratch_shapes=[pltpu.SemaphoreType.DMA((MOVES * MAXP,))],
        compiler_params=LIMIT,
        cost_estimate=cost(4_000_000 // HALVES),
    )(plan, pool.reshape(POOL, MAXP, HALVES, PR, HD))


def cross_kernel(cap, plan_ref, held_ref, out_ref):
    @pl.loop(0, cap, step=8)
    def _(base):
        for i in range(8):
            out_ref[base + i] = held_ref[plan_ref[0, base + i]]


def crossing(plan, held, cap):
    return pl.pallas_call(
        functools.partial(cross_kernel, cap),
        out_shape=jax.ShapeDtypeStruct((cap, PR, HD), jnp.bfloat16),
        in_specs=[spec(SMEM), spec(VMEM)],
        out_specs=spec(VMEM),
        compiler_params=LIMIT,
        cost_estimate=cost(4_000_000 // HALVES),
    )(plan, held)


def deliver_kernel(cap, plan_ref, held_ref, crossed_ref, out_ref):
    @pl.loop(0, PIECES, step=8)
    def _(base):
        for i in range(8):
            origin = plan_ref[1, base + i]
            kept = held_ref[jnp.minimum(origin, PIECES - 1)]
            crossed = crossed_ref[jnp.clip(origin - PIECES, 0, cap - 1)]
            out_ref[base + i] = jnp.where(origin < PIECES, kept, crossed)


def deliver(plan, held, crossed, cap):
    return pl.pallas_call(
        functools.partial(deliver_kernel, cap),
        out_shape=jax.ShapeDtypeStruct((PIECES, PR, HD), jnp.bfloat16),
        in_specs=[spec(SMEM), spec(VMEM), spec(VMEM)],
        out_specs=spec(VMEM),
        compiler_params=LIMIT,
        cost_estimate=cost(6_000_000 // HALVES),
    )(plan, held, crossed)


def place_pages(plan_ref, pool_ref, received_refs, out_ref):
    out_ref[...] = pool_ref[...]

    @pl.loop(0, MOVES)
    def _(k):
        for j in range(MAXP):
            page = plan_ref[3, k * MAXP + j]
            for quarter in range(MAXP):
                for part, received_ref in enumerate(received_refs):
                    first = (quarter * HALVES + part) * PR
                    out_ref[page, first : first + PR, :] = received_ref[MAXP * j + quarter, k]


def keys_kernel(own_ref, plan_ref, table_ref, lengths_ref, qkv_ref, pool_ref, *refs):
    received_refs, (moved_ref, cache_ref, fresh_ref) = refs[:HALVES], refs[HALVES:]
    place_pages(plan_ref, pool_ref, received_refs, moved_ref)
    scale = 1.0 / math.sqrt(HD)
    position = lax.broadcasted_iota(jnp.int32, (16, MAXP * PAGE), 1)
    fresh_index = lax.broadcasted_iota(jnp.int32, (16, 16), 1)
    step = lax.broadcasted_iota(jnp.int32, (16, 16), 0) & 1
    by_rows = (((1,), (1,)), ((), ()))

    @pl.loop(0, ROWS, step=4)
    def _(base):
        for i in range(4):
            r = base + i
            queries = qkv_ref[r, 0:16, :]
            scores = jnp.concatenate(
                [
                    lax.dot_general(
                        queries,
                        moved_ref[table_ref[r, j]],
                        by_rows,
                        preferred_element_type=jnp.float32,
                    )
                    for j in range(MAXP)
                ],
                axis=1,
            )
            length = lengths_ref[own_ref[0] * ROWS + r]
            scores = jnp.where(position < length, scores * scale, -jnp.inf)
            fresh = lax.dot_general(
                queries, qkv_ref[r, 16:32, :], by_rows, preferred_element_type=jnp.float32
            )
            fresh = jnp.where(fresh_index <= step, fresh * scale, -jnp.inf)
            top = jnp.maximum(
                jnp.max(scores, axis=1, keepdims=True), jnp.max(fresh, axis=1, keepdims=True)
            )
            scores = jnp.exp(scores - top)
            fresh = jnp.exp(fresh - top)
            total = jnp.sum(scores, axis=1, keepdims=True) + jnp.sum(fresh, axis=1, keepdims=True)
            cache_ref[r] = (scores / total).astype(jnp.bfloat16)
            fresh_ref[r] = (fresh / total).astype(jnp.bfloat16)


def keys_step(own, plan, table, lengths, qkv, pool, received):
    return pl.pallas_call(
        keys_kernel,
        out_shape=(
            jax.ShapeDtypeStruct((POOL, PAGE, HD), jnp.bfloat16),
            jax.ShapeDtypeStruct((ROWS, 16, MAXP * PAGE), jnp.bfloat16),
            jax.ShapeDtypeStruct((ROWS, 16, 16), jnp.bfloat16),
        ),
        in_specs=[spec(SMEM)] * 4 + [spec(VMEM)] * (2 + HALVES),
        out_specs=(spec(VMEM),) * 3,
        compiler_params=LIMIT,
        cost_estimate=cost(16_000_000),
    )(own, plan, table, lengths, qkv, pool, *received)


def values_kernel(plan_ref, table_ref, cache_ref, fresh_ref, qkv_ref, pool_ref, *refs):
    received_refs, (moved_ref, out_ref) = refs[:HALVES], refs[HALVES:]
    place_pages(plan_ref, pool_ref, received_refs, moved_ref)
    for r in range(ROWS):
        mixed = jnp.dot(fresh_ref[r], qkv_ref[r, 32:48, :], preferred_element_type=jnp.float32)
        for j in range(MAXP):
            mixed += jnp.dot(
                cache_ref[r, :, j * PAGE : (j + 1) * PAGE],
                moved_ref[table_ref[r, j]],
                preferred_element_type=jnp.float32,
            )
        out_ref[r // 2, r % 2] = mixed.astype(jnp.bfloat16)


def values_step(plan, table, weights, fresh, qkv, pool, received):
    return pl.pallas_call(
        values_kernel,
        out_shape=(
            jax.ShapeDtypeStruct((POOL, PAGE, HD), jnp.bfloat16),
            jax.ShapeDtypeStruct((TP, 2, 16, HD), jnp.bfloat16),
        ),
        in_specs=[spec(SMEM)] * 2 + [spec(VMEM)] * (4 + HALVES),
        out_specs=(spec(VMEM),) * 2,
        compiler_params=LIMIT,
        cost_estimate=cost(12_000_000),
    )(plan, table, weights, fresh, qkv, pool, *received)


def swap(array, axes):
    return lax.all_to_all(array, axes, split_axis=0, concat_axis=0, tiled=True)


def move_and_attend(cap, own, plan, table, lengths, qkv, key_pool, value_pool):
    chunks = [(pool, part) for pool in (key_pool, value_pool) for part in range(HALVES)]
    held, crossed, received = [], [], []
    for pool, part in chunks:
        send = outgoing(plan, pool, part)
        if held:
            send, held[-1] = lax.optimization_barrier((send, held[-1]))
        held.append(swap(send, ("y", "x")).reshape(PIECES, PR, HD))
    for piece in held:
        leaving = crossing(plan, piece, cap)
        crossed.append(lax.ppermute(leaving, "zh", [(0, 1), (1, 0)]))
    for piece, other in zip(held, crossed):
        final = deliver(plan, piece, other, cap).reshape(SPREAD, MOVES, PR, HD)
        received.append(swap(final, ("y", "x")))
    key_moved, weights, fresh = keys_step(
        own, plan, table, lengths, qkv, key_pool, received[:HALVES]
    )
    value_moved, mixed = values_step(
        plan, table, weights, fresh, qkv, value_pool, received[HALVES:]
    )
    return mixed, key_moved, value_moved


def body(
    new_queries,
    new_keys,
    new_values,
    key_pool,
    value_pool,
    lengths,
    page_table,
    mig_row,
    mig_source,
    mig_pages,
):
    own = lax.axis_index(("y", "zh", "x")).astype(jnp.int32).reshape(1)
    plan = make_plan(own, mig_row, mig_source, mig_pages, page_table)
    qkv = swap(pack(new_queries, new_keys, new_values), ("zl", "c")).reshape(ROWS, QKV, HD)
    count = plan[5, 0]
    branch = sum((count > cap).astype(jnp.int32) for cap in CAPS[:-1])
    mixed, key_moved, value_moved = lax.switch(
        branch,
        [functools.partial(move_and_attend, cap) for cap in CAPS],
        own,
        plan,
        page_table,
        lengths,
        qkv,
        key_pool,
        value_pool,
    )
    attention = unpack(swap(mixed, ("zl", "c")))
    return (attention, key_moved, value_moved)


def solution(mesh):
    fine = Mesh(mesh.devices.reshape(4, NZ, NX, 4, 2), ("y", "zh", "x", "zl", "c"))
    inst, tp = ("y", "zh", "x"), ("zl", "c")
    rows = P(inst + tp, None, None)
    pool = P(inst, None, tp)
    return jax.shard_map(
        body,
        mesh=fine,
        in_specs=(rows, rows, rows, pool, pool, P(), P(inst, None), P(), P(), P()),
        out_specs=(rows, pool, pool),
        check_vma=False,
    )
```

time: 318 us -> 186 us (0.58)
  local copies, waits for them, and re-layouts: 109 us -> 9.07 us
  blocking collectives: 76.1 us -> 35 us
  Pallas kernels: 0 us -> 21.9 us
  waiting for transfers between devices: 51.9 us -> 73.7 us
  starting transfers between devices: 60.4 us -> 42.8 us
  other arithmetic: 12.7 us -> 0 us
  matrix products: 5.04 us -> 0 us
    scatter x5 -> x0, local copies, waits for them, and re-layouts: 41.6 us -> none  [the longest x1 17.9 us: migrate_pages(): key_pool.at[destination].set(key_recv.reshape(flat_shape), mode='drop')]
    ppermute x0 -> x2, waiting for transfers between devices: none -> 41.3 us  [move_and_attend(): crossed.append(lax.ppermute(leaving, 'zh', [(0, 1), (1, 0)]))]
    all_to_all x1, blocking collectives: 76.1 us -> 35 us  [swap(): return lax.all_to_all(array, axes, split_axis=0, concat_axis=0, tiled=True)]
    unnamed x37 -> x8, local copies, waits for them, and re-layouts: 35.9 us -> 3.8 us
    all_to_all x5, starting transfers between devices: 60.4 us -> 32.6 us  [swap(): return lax.all_to_all(array, axes, split_axis=0, concat_axis=0, tiled=True)]
    pallas_call x0 -> x11, Pallas kernels: none -> 21.9 us  [the longest x1 5.19 us: keys_step(): pl.pallas_call(keys_kernel, out_shape=(jax.ShapeDtypeStruct((POOL, PAGE,...]
    all_to_all x5, waiting for transfers between devices: 51.9 us -> 32.4 us  [swap(): return lax.all_to_all(array, axes, split_axis=0, concat_axis=0, tiled=True)]
    gather x9 -> x0, local copies, waits for them, and re-layouts: 12.3 us -> none  [the longest x1 3.72 us: body(): key_moved[page_table]]
  transfers between devices with their start and end apart: 5 -> 7, of which waited for: 2 -> 5; matrix products, arithmetic and copies ran while one was open for 33% -> 2% of each run, Pallas kernels for 0% -> 7%
where the time goes in v1:
time: 186 us; the launch traced here: 185 us
  waiting for transfers between devices  73.7 us (40%)
  starting transfers between devices  42.8 us (23%)
  blocking collectives  35 us (19%)
  Pallas kernels  21.9 us (12%)
  local copies, waits for them, and re-layouts  9.07 us (5%)
  between operations  2.63 us (1%)
    ppermute x2, waiting for transfers between devices, move_and_attend(): crossed.append(lax.ppermute(leaving, 'zh', [(0, 1), (1, 0)]))  41.3 us
    all_to_all x1, blocking collectives, swap(): return lax.all_to_all(array, axes, split_axis=0, concat_axis=0, tiled=True)  35 us
    all_to_all x5, starting transfers between devices, swap(): return lax.all_to_all(array, axes, split_axis=0, concat_axis=0, tiled=True)  32.6 us
    all_to_all x5, waiting for transfers between devices, swap(): return lax.all_to_all(array, axes, split_axis=0, concat_axis=0, tiled=True)  32.4 us
    ppermute x2, starting transfers between devices, move_and_attend(): crossed.append(lax.ppermute(leaving, 'zh', [(0, 1), (1, 0)]))  10.2 us
    pallas_call x1, Pallas kernels, keys_step(): pl.pallas_call(keys_kernel, out_shape=(jax.ShapeDtypeStruct((POOL, PAGE,...  5.19 us
    pallas_call x2, Pallas kernels, outgoing(): pl.pallas_call(functools.partial(send_kernel, part), out_shape=jax.ShapeD...  5.17 us
    unnamed x8, local copies, waits for them, and re-layouts  3.8 us
  transfers between devices with their start and end apart: 7, of which 5 were waited for; matrix products, arithmetic and copies ran while one was open for 2% of the time, Pallas kernels for 7%

profile of v1, /device:TPU:1, one launch (start us, length us, event | category | flops | bytes accessed | tf_op | source)
XLA Modules:
  0.0 185.3 jit_solution(1469244826672084443)
XLA Ops:
  0.6 0.8 copy-done.12
  1.5 0.7 copy-done.13
  2.2 0.7 copy-done.14
  2.9 0.8 shard_map.122
  3.6 7.4 %all-to-all-start.16 = ((bf16[8,2,48,128]{3,2,1,0:T(8,128)(2,1)}), bf16[8,2,48,128]{3,2,1,0:T(8,128)(2,1)}, u32[]{:S(2)}, u32[]{:S(2)}) async-start(bf16[8,2,48,128]{3,2,1,0:T(8,128)(2,1)} %shard_map.122), calls=%async_computation.16 | async-start | bytes 393216 | tf_op jit(solution)/shard_map/all_to_all | solution.py:327
  11.0 0.7 reshape.102.row_ref
  12.4 0.8 copy.14.table_ref
  13.2 0.8 copy.13.pages_ref
  14.0 0.8 shard_map.121
  17.6 132.0 %conditional.1 = (bf16[8,2,16,128]{3,2,1,0:T(8,128)(2,1)S(1)}, bf16[64,128,128]{2,1,0:T(8,128)(2,1)}, bf16[64,128,128]{2,1,0:T(8,128)(2,1)}) conditional(s32[]{:T(128)} %bitcast.25, (bf16[64,128,128]{2,1,0:T(8,128)(2,1)}, s32[8,256]{1,0:T(8,128)S(1)}, bf16[64,128,128]{2,1,0:T(8,128)(2,1)}, s32[1]{0:T(128)}, ...), branch_computations={%region_0.0_spmd, %region_1.0_spmd, %region_2.0_spmd, %region_3.0_... | conditional | bytes 111322544 | solution.py:370
  17.6 3.4 %branch_0_fun.9 = bf16[16,11,32,128]{3,2,1,0:T(8,128)(2,1)} custom-call(s32[8,256]{1,0:T(8,128)S(1)} %get-tuple-element.56.plan_ref, bf16[64,4,1,32,128]{4,3,2,1,0:T(8,128)(2,1)} %bitcast.51), custom_call_target="tpu_custom_call" | custom-call | bytes 4000000 | tf_op jit(solution)/shard_map/cond/branch_0_fun/pallas_call | solution.py:178
  21.1 6.9 %all-to-all-start = ((bf16[16,11,32,128]{3,2,1,0:T(8,128)(2,1)}), bf16[16,11,32,128]{3,2,1,0:T(8,128)(2,1)S(1)}, u32[]{:S(2)}, u32[]{:S(2)}) async-start(bf16[16,11,32,128]{3,2,1,0:T(8,128)(2,1)} %branch_0_fun.9), calls=%async_computation | async-start | bytes 2883584 | tf_op jit(solution)/shard_map/cond/branch_0_fun/all_to_all | solution.py:327
  28.0 1.7 branch_0_fun.8
  29.7 1.1 copy-done.1
  30.8 16.1 %all-to-all-done = bf16[16,11,32,128]{3,2,1,0:T(8,128)(2,1)S(1)} async-done(((bf16[16,11,32,128]{3,2,1,0:T(8,128)(2,1)}), bf16[16,11,32,128]{3,2,1,0:T(8,128)(2,1)S(1)}, u32[]{:S(2)}, u32[]{:S(2)}) %all-to-all-start) | async-done | bytes 1441824 | tf_op jit(solution)/shard_map/cond/branch_0_fun/all_to_all | solution.py:327
  47.0 5.1 %all-to-all-start.2 = ((bf16[16,11,32,128]{3,2,1,0:T(8,128)(2,1)}), bf16[16,11,32,128]{3,2,1,0:T(8,128)(2,1)S(1)}, u32[]{:S(2)}, u32[]{:S(2)}) async-start(bf16[16,11,32,128]{3,2,1,0:T(8,128)(2,1)} %copy-done.1), calls=%async_computation.2 | async-start | bytes 2883584 | tf_op jit(solution)/shard_map/cond/branch_0_fun/all_to_all | solution.py:327
  52.0 0.9 branch_0_fun.10
  53.0 5.0 %collective-permute-start = (bf16[96,32,128]{2,1,0:T(8,128)(2,1)S(1)}, bf16[96,32,128]{2,1,0:T(8,128)(2,1)S(1)}, u32[]{:S(2)}, u32[]{:S(2)}) collective-permute-start(bf16[96,32,128]{2,1,0:T(8,128)(2,1)S(1)} %branch_0_fun.10), channel_id=1, source_target_pairs={{0,32},{32,0},{1,33},{33,1},{2,34},{34,2},{3,35},{35,3},{4,36},{36... | collective-permute-start | bytes 2359304 | tf_op jit(solution)/shard_map/cond/branch_0_fun/ppermute | solution.py:340
  58.0 15.6 %collective-permute-done.crossed_ref = bf16[96,32,128]{2,1,0:T(8,128)(2,1)S(1)} collective-permute-done((bf16[96,32,128]{2,1,0:T(8,128)(2,1)S(1)}, bf16[96,32,128]{2,1,0:T(8,128)(2,1)S(1)}, u32[]{:S(2)}, u32[]{:S(2)}) %collective-permute-start) | collective-permute-done | bytes 786464 | tf_op jit(solution)/shard_map/cond/branch_0_fun/ppermute | solution.py:340
  73.6 1.8 branch_0_fun.11
  75.5 1.1 copy-done
  76.6 6.4 %all-to-all-start.1 = ((bf16[16,11,32,128]{3,2,1,0:T(8,128)(2,1)}), bf16[16,11,32,128]{3,2,1,0:T(8,128)(2,1)S(1)}, u32[]{:S(2)}, u32[]{:S(2)}) async-start(bf16[16,11,32,128]{3,2,1,0:T(8,128)(2,1)} %bitcast.43), calls=%async_computation.1 | async-start | bytes 2883584 | tf_op jit(solution)/shard_map/cond/branch_0_fun/all_to_all | solution.py:327
  83.0 0.9 branch_0_fun.13
  83.9 5.2 %collective-permute-start.1 = (bf16[96,32,128]{2,1,0:T(8,128)(2,1)S(1)}, bf16[96,32,128]{2,1,0:T(8,128)(2,1)S(1)}, u32[]{:S(2)}, u32[]{:S(2)}) collective-permute-start(bf16[96,32,128]{2,1,0:T(8,128)(2,1)S(1)} %branch_0_fun.13), channel_id=1, source_target_pairs={{0,32},{32,0},{1,33},{33,1},{2,34},{34,2},{3,35},{35,3},{4,36},{36... | collective-permute-start | bytes 2359304 | tf_op jit(solution)/shard_map/cond/branch_0_fun/ppermute | solution.py:340
  89.1 25.7 %collective-permute-done.1.crossed_ref = bf16[96,32,128]{2,1,0:T(8,128)(2,1)S(1)} collective-permute-done((bf16[96,32,128]{2,1,0:T(8,128)(2,1)S(1)}, bf16[96,32,128]{2,1,0:T(8,128)(2,1)S(1)}, u32[]{:S(2)}, u32[]{:S(2)}) %collective-permute-start.1) | collective-permute-done | bytes 786464 | tf_op jit(solution)/shard_map/cond/branch_0_fun/ppermute | solution.py:340
  114.8 1.8 branch_0_fun.14
  116.6 1.1 copy-done.4
  117.8 6.8 %all-to-all-start.3 = ((bf16[16,11,32,128]{3,2,1,0:T(8,128)(2,1)}), bf16[16,11,32,128]{3,2,1,0:T(8,128)(2,1)S(1)}, u32[]{:S(2)}, u32[]{:S(2)}) async-start(bf16[16,11,32,128]{3,2,1,0:T(8,128)(2,1)} %bitcast.44), calls=%async_computation.3 | async-start | bytes 2883584 | tf_op jit(solution)/shard_map/cond/branch_0_fun/all_to_all | solution.py:327
  124.7 5.2 %branch_0_fun.12 = (bf16[64,128,128]{2,1,0:T(8,128)(2,1)}, bf16[16,16,512]{2,1,0:T(8,128)(2,1)S(1)}, bf16[16,16,16]{2,1,0:T(8,128)(2,1)S(1)}) custom-call(s32[1]{0:T(128)} %get-tuple-element.58.own_ref, s32[8,256]{1,0:T(8,128)S(1)} %get-tuple-element.56.plan_ref, s32[16,4]{1,0:T(8,128)S(1)} %copy.15.table_ref, s32[512]{0:T(512)S(1)} %copy-done.27, ...), custom_call_target="tpu_custom_call" | custom-call | bytes 16000000 | tf_op jit(solution)/shard_map/cond/branch_0_fun/pallas_call | solution.py:284
  129.8 16.0 %all-to-all-done.3.refs_0_ = bf16[16,11,32,128]{3,2,1,0:T(8,128)(2,1)S(1)} async-done(((bf16[16,11,32,128]{3,2,1,0:T(8,128)(2,1)}), bf16[16,11,32,128]{3,2,1,0:T(8,128)(2,1)S(1)}, u32[]{:S(2)}, u32[]{:S(2)}) %all-to-all-start.3) | async-done | bytes 1441824 | tf_op jit(solution)/shard_map/cond/branch_0_fun/all_to_all | solution.py:327
  145.8 3.8 %branch_0_fun.15 = (bf16[64,128,128]{2,1,0:T(8,128)(2,1)}, bf16[8,2,16,128]{3,2,1,0:T(8,128)(2,1)S(1)}) custom-call(s32[8,256]{1,0:T(8,128)S(1)} %get-tuple-element.56.plan_ref, s32[16,4]{1,0:T(8,128)S(1)} %copy.15.table_ref, bf16[16,16,512]{2,1,0:T(8,128)(2,1)S(1)} %get-tuple-element.64.cache_ref, bf16[16,16,16]{2,1,0:T(8,128)(2,1)S(1)} %get-tuple-element.65.fresh_ref, ...), custom_call_target="tpu_custom_call" | custom-call | bytes 12000000 | tf_op jit(solution)/shard_map/cond/branch_0_fun/pallas_call | solution.py:313
  149.6 35.0 %all_to_all.74.in_ref = bf16[8,2,16,128]{3,2,1,0:T(8,128)(2,1)S(1)} all-to-all(bf16[8,2,16,128]{3,2,1,0:T(8,128)(2,1)S(1)} %get-tuple-element.118), channel_id=1, replica_groups=mesh['y'=4,'zh'=2,'x'=4,'zl'=4,'c'=2] {'zl','c'}, dimensions={0} | all-to-all | bytes 131072 | tf_op jit(solution)/shard_map/all_to_all | solution.py:327
  (21 shorter events, 2.3 us)
Async XLA Ops:
  0.6 0.8 copy-start.12
  1.5 0.7 copy-start.13
  2.2 0.7 copy-start.14
  3.6 14.0 %all-to-all-start.16 = ((bf16[8,2,48,128]{3,2,1,0:T(8,128)(2,1)}), bf16[8,2,48,128]{3,2,1,0:T(8,128)(2,1)}, u32[]{:S(2)}, u32[]{:S(2)}) async-start(bf16[8,2,48,128]{3,2,1,0:T(8,128)(2,1)} %shard_map.122), calls=%async_computation.16 | async-start | bytes 393216 | tf_op jit(solution)/shard_map/all_to_all | solution.py:327
  21.0 6.9 %copy-start.15 = (bf16[64,128,128]{2,1,0:T(8,128)(2,1)S(1)}, bf16[64,128,128]{2,1,0:T(8,128)(2,1)}, u32[]{:S(2)}) copy-start(bf16[64,128,128]{2,1,0:T(8,128)(2,1)} %get-tuple-element.62.pool_ref) | copy-start | bytes 6291460 | tf_op jit(solution)/shard_map/cond
  21.1 25.9 %all-to-all-start = ((bf16[16,11,32,128]{3,2,1,0:T(8,128)(2,1)}), bf16[16,11,32,128]{3,2,1,0:T(8,128)(2,1)S(1)}, u32[]{:S(2)}, u32[]{:S(2)}) async-start(bf16[16,11,32,128]{3,2,1,0:T(8,128)(2,1)} %branch_0_fun.9), calls=%async_computation | async-start | bytes 2883584 | tf_op jit(solution)/shard_map/cond/branch_0_fun/all_to_all | solution.py:327
  29.7 1.1 copy-start.1
  47.0 29.6 %all-to-all-start.2 = ((bf16[16,11,32,128]{3,2,1,0:T(8,128)(2,1)}), bf16[16,11,32,128]{3,2,1,0:T(8,128)(2,1)S(1)}, u32[]{:S(2)}, u32[]{:S(2)}) async-start(bf16[16,11,32,128]{3,2,1,0:T(8,128)(2,1)} %copy-done.1), calls=%async_computation.2 | async-start | bytes 2883584 | tf_op jit(solution)/shard_map/cond/branch_0_fun/all_to_all | solution.py:327
  53.0 20.6 %collective-permute-start = (bf16[96,32,128]{2,1,0:T(8,128)(2,1)S(1)}, bf16[96,32,128]{2,1,0:T(8,128)(2,1)S(1)}, u32[]{:S(2)}, u32[]{:S(2)}) collective-permute-start(bf16[96,32,128]{2,1,0:T(8,128)(2,1)S(1)} %branch_0_fun.10), channel_id=1, source_target_pairs={{0,32},{32,0},{1,33},{33,1},{2,34},{34,2},{3,35},{35,3},{4,36},{36... | collective-permute-start | bytes 2359304 | tf_op jit(solution)/shard_map/cond/branch_0_fun/ppermute | solution.py:340
  75.4 1.1 copy-start
  76.6 41.2 %all-to-all-start.1 = ((bf16[16,11,32,128]{3,2,1,0:T(8,128)(2,1)}), bf16[16,11,32,128]{3,2,1,0:T(8,128)(2,1)S(1)}, u32[]{:S(2)}, u32[]{:S(2)}) async-start(bf16[16,11,32,128]{3,2,1,0:T(8,128)(2,1)} %bitcast.43), calls=%async_computation.1 | async-start | bytes 2883584 | tf_op jit(solution)/shard_map/cond/branch_0_fun/all_to_all | solution.py:327
  83.9 30.9 %collective-permute-start.1 = (bf16[96,32,128]{2,1,0:T(8,128)(2,1)S(1)}, bf16[96,32,128]{2,1,0:T(8,128)(2,1)S(1)}, u32[]{:S(2)}, u32[]{:S(2)}) collective-permute-start(bf16[96,32,128]{2,1,0:T(8,128)(2,1)S(1)} %branch_0_fun.13), channel_id=1, source_target_pairs={{0,32},{32,0},{1,33},{33,1},{2,34},{34,2},{3,35},{35,3},{4,36},{36... | collective-permute-start | bytes 2359304 | tf_op jit(solution)/shard_map/cond/branch_0_fun/ppermute | solution.py:340
  116.6 1.1 copy-start.4
  117.7 6.8 %copy-start.23 = (s32[16,4]{0,1:T(4,128)S(1)}, s32[16,4]{0,1:T(4,128)}, u32[]{:S(2)}) copy-start(s32[16,4]{0,1:T(4,128)} %get-tuple-element.125) | copy-start | bytes 772 | tf_op jit(solution)/shard_map/cond
  117.7 6.9 %copy-start.19 = (bf16[16,48,128]{2,1,0:T(8,128)(2,1)S(1)}, bf16[16,48,128]{2,1,0:T(8,128)(2,1)}, u32[]{:S(2)}) copy-start(bf16[16,48,128]{2,1,0:T(8,128)(2,1)} %get-tuple-element.60.qkv_ref) | copy-start | bytes 589828 | tf_op jit(solution)/shard_map/cond
  117.7 6.9 %copy-start.27 = (s32[512]{0:T(512)S(1)}, s32[512]{0:T(512)}, u32[]{:S(2)}) copy-start(s32[512]{0:T(512)} %get-tuple-element.59.lengths_ref) | copy-start | bytes 6148 | tf_op jit(solution)/shard_map/cond
  117.8 28.1 %all-to-all-start.3 = ((bf16[16,11,32,128]{3,2,1,0:T(8,128)(2,1)}), bf16[16,11,32,128]{3,2,1,0:T(8,128)(2,1)S(1)}, u32[]{:S(2)}, u32[]{:S(2)}) async-start(bf16[16,11,32,128]{3,2,1,0:T(8,128)(2,1)} %bitcast.44), calls=%async_computation.3 | async-start | bytes 2883584 | tf_op jit(solution)/shard_map/cond/branch_0_fun/all_to_all | solution.py:327
